TPU v7x, 128 devices: a whole 4x4x4 slice. The times are simulated.
128 devices in a mesh: tm: 64 (over z, y, x), blk: 2 (over core).
Axes of the slice: x: 4, y: 4, z: 4, core: 2. Of those that a mesh axis runs over, the one named last changes fastest.
Arguments:
- diag_block: float32 [128, 1024, 1024], P('tm', 'blk'), may hold values from -24.5 to 25.25, as said below
- coupling: float32 [128, 1024, 1024], P('tm', 'blk'), may hold values from -12.25 to 12.25
- arrow: float32 [128, 64, 1024], P('tm', 'blk'), may hold values from -0.125 to 0.125
- corner: float32 [64, 64], P('blk'), may hold values from -6 to 6
Outputs:
- inner_pivot: float32 [64, 1024, 1024], P('tm', 'blk')
- inner_left: float32 [64, 1024, 1024], P('tm', 'blk')
- inner_right: float32 [64, 1024, 1024], P('tm', 'blk')
- inner_arrow: float32 [64, 64, 1024], P('tm', 'blk')
- pivot: float32 [64, 1024, 1024], P('tm', 'blk')
- left_factor_even: float32 [64, 1024, 1024], P('tm', 'blk')
- right_factor_even: float32 [64, 1024, 1024], P('tm', 'blk')
- arrow_factor_even: float32 [64, 64, 1024], P('tm', 'blk')
- corner_out: float32 [64, 64], P('blk')
Inputs may be any that keep to these rules, and one draw needn't show every extreme that they name: `diag_block`: Symmetric; together with the coupling blocks the matrix of all day blocks is positive definite.
All inputs are finite; a program needn't handle non-finite values.
Results may differ from a plain program's by a relative error of at most 0.00014.
Values sent between devices are 32-bit elements; how exact they have to be, the bound alone decides.
A program may use at most 128 MiB of HBM per device.

v0:
```python
import jax
import jax.numpy as jnp
from jax import lax
from jax.sharding import PartitionSpec as P


def shifted(value, axis, steps):
    count = lax.axis_size(axis)
    leading, last = (max(0, -steps), min(count, count - steps))
    return lax.ppermute(value, axis, [(source, source + steps) for source in range(leading, last)])


def transposed_product(left, right):
    return lax.dot_general(
        left,
        right,
        (((0,), (0,)), ((), ())),
        precision=lax.Precision.HIGHEST,
        preferred_element_type=jnp.float32,
    )


def eliminate(pivot_rows, first, second, arrow_piece):
    member = lax.axis_index("blk")
    row_share = pivot_rows.shape[0]
    node_count = pivot_rows.shape[1]
    whole_pivot = lax.all_gather(pivot_rows, "blk", axis=0, tiled=True)
    factor = jnp.linalg.cholesky(whole_pivot)
    right_hand = jnp.concatenate([first.T, second.T, arrow_piece.T], axis=1)
    solved = jax.scipy.linalg.solve_triangular(factor, right_hand, lower=True)
    own_first = solved[:, :row_share]
    own_second = solved[:, row_share : 2 * row_share]
    own_arrow = solved[:, 2 * row_share :]
    full_first, full_second, full_arrow = (
        lax.all_gather(own_first, "blk", axis=1, tiled=True),
        lax.all_gather(own_second, "blk", axis=1, tiled=True),
        lax.all_gather(own_arrow, "blk", axis=1, tiled=True),
    )
    own_factor = lax.dynamic_slice_in_dim(factor, member * row_share, row_share, 0)
    left_side = jnp.concatenate([own_first, own_second, own_arrow], axis=1)
    right_side = jnp.concatenate([full_first, full_second, full_arrow], axis=1)
    product = transposed_product(left_side, right_side)
    first_rows = product[:row_share]
    second_rows = product[row_share : 2 * row_share]
    arrow_part = product[2 * row_share :]
    blocks = (
        first_rows[:, :node_count],
        first_rows[:, node_count : 2 * node_count],
        second_rows[:, :node_count],
        second_rows[:, node_count : 2 * node_count],
        arrow_part[:, :node_count],
        arrow_part[:, node_count : 2 * node_count],
        arrow_part[:, 2 * node_count :],
    )
    return (own_factor, own_first, own_second, own_arrow, blocks)


def local(diag_block, coupling, arrow, corner):
    partition_count = lax.axis_size("tm")
    position = lax.axis_index("tm")
    open_end = (position < partition_count - 1).astype(jnp.float32)
    forward = coupling[1] * open_end
    backward = lax.all_to_all(coupling[0].T, "blk", split_axis=0, concat_axis=1, tiled=True)
    inner_factor, sep_cols, next_cols, arrow_cols, blocks = eliminate(
        diag_block[1], backward, forward, arrow[1]
    )
    (
        first_first,
        first_second,
        second_first,
        second_second,
        arrow_first,
        arrow_second,
        arrow_arrow,
    ) = blocks
    received_schur, received_left, received_arrow = shifted(
        (second_second, -first_second, arrow_second), "tm", 1
    )
    pivot_out = diag_block[0] - first_first - received_schur
    right_out = -second_first
    arrow_out = arrow[0] - arrow_first - received_arrow
    corner_out = corner - lax.psum(arrow_arrow, "tm")
    return (
        inner_factor[None],
        sep_cols.T[None],
        next_cols.T[None],
        arrow_cols.T[None],
        pivot_out[None],
        received_left[None],
        right_out[None],
        arrow_out[None],
        corner_out,
    )


def solution(mesh):
    placed = (P("tm", "blk", None), P("tm", "blk", None), P("tm", "blk", None), P("blk", None))
    return jax.shard_map(
        local,
        mesh=mesh,
        in_specs=placed,
        out_specs=(
            P("tm", "blk", None),
            P("tm", "blk", None),
            P("tm", "blk", None),
            P("tm", "blk", None),
            P("tm", "blk", None),
            P("tm", "blk", None),
            P("tm", "blk", None),
            P("tm", "blk", None),
            P("blk", None),
        ),
        check_vma=False,
    )
```

profile of v0, /device:TPU:0, one launch (start us, length us, event | category | flops | bytes accessed | tf_op | source)
XLA Modules:
  0.0 922.3 jit_solution(9518008110012547831)
XLA Ops:
  8.8 1.8 copy.24
  10.6 4.1 slice_bitcast_fusion
  14.7 1.8 copy.21
  16.5 3.8 all-to-all-start
  20.4 2.8 all-to-all-done
  23.2 1.8 copy.22
  25.0 2.1 copy.23
  27.1 4.2 pad_maximum_fusion
  31.3 5.5 copy.20
  36.8 4.4 fusion.6
  41.2 2.0 copy-done
  43.2 11.7 %cholesky.223 = f32[128,128]{1,0:T(8,128)S(1)} custom-call(f32[128,128]{1,0:T(8,128)S(1)} %cholesky.580), custom_call_target="Cholesky" | custom-call | tf_op jit(solution)/shard_map/jit(cholesky)/cholesky | solution.py:28
  55.0 9.8 %custom-call.63 = f32[1,128,128]{1,2,0:T(8,128)S(1)} custom-call(f32[1,128,128]{2,1,0:T(8,128)S(1)} %get-tuple-element.86), custom_call_target="InvertDiagBlocksLowerTriangular" | custom-call | tf_op jit(solution)/shard_map/jit(cholesky)/cholesky | solution.py:28
  64.8 2.5 cholesky.255
  67.3 2.3 constant_dynamic-update-slice_fusion.32
  71.2 11.9 %cholesky.244 = f32[128,128]{1,0:T(8,128)S(1)} custom-call(f32[128,128]{1,0:T(8,128)S(1)} %cholesky.584), custom_call_target="Cholesky" | custom-call | tf_op jit(solution)/shard_map/jit(cholesky)/cholesky | solution.py:28
  83.7 9.8 %custom-call.64 = f32[1,128,128]{1,2,0:T(8,128)S(1)} custom-call(f32[1,128,128]{2,1,0:T(8,128)S(1)} %get-tuple-element.83), custom_call_target="InvertDiagBlocksLowerTriangular" | custom-call | tf_op jit(solution)/shard_map/jit(cholesky)/cholesky | solution.py:28
  94.8 2.1 convolution_subtract_fusion.8
  96.9 11.7 %cholesky.468 = f32[128,128]{1,0:T(8,128)S(1)} custom-call(f32[128,128]{1,0:T(8,128)S(1)} %cholesky.589), custom_call_target="Cholesky" | custom-call | tf_op jit(solution)/shard_map/jit(cholesky)/cholesky | solution.py:28
  109.9 9.8 %custom-call.65 = f32[1,128,128]{1,2,0:T(8,128)S(1)} custom-call(f32[1,128,128]{2,1,0:T(8,128)S(1)} %get-tuple-element.80), custom_call_target="InvertDiagBlocksLowerTriangular" | custom-call | tf_op jit(solution)/shard_map/jit(cholesky)/cholesky | solution.py:28
  120.9 2.3 convolution_subtract_fusion.9
  123.2 12.1 %cholesky.487 = f32[128,128]{1,0:T(8,128)S(1)} custom-call(f32[128,128]{1,0:T(8,128)S(1)} %cholesky.594), custom_call_target="Cholesky" | custom-call | tf_op jit(solution)/shard_map/jit(cholesky)/cholesky | solution.py:28
  136.6 9.8 %custom-call.66 = f32[1,128,128]{1,2,0:T(8,128)S(1)} custom-call(f32[1,128,128]{2,1,0:T(8,128)S(1)} %get-tuple-element.77), custom_call_target="InvertDiagBlocksLowerTriangular" | custom-call | tf_op jit(solution)/shard_map/jit(cholesky)/cholesky | solution.py:28
  147.5 2.3 convolution_subtract_fusion.10
  149.9 11.7 %cholesky.506 = f32[128,128]{1,0:T(8,128)S(1)} custom-call(f32[128,128]{1,0:T(8,128)S(1)} %cholesky.599), custom_call_target="Cholesky" | custom-call | tf_op jit(solution)/shard_map/jit(cholesky)/cholesky | solution.py:28
  162.9 9.9 %custom-call.67 = f32[1,128,128]{1,2,0:T(8,128)S(1)} custom-call(f32[1,128,128]{2,1,0:T(8,128)S(1)} %get-tuple-element.74), custom_call_target="InvertDiagBlocksLowerTriangular" | custom-call | tf_op jit(solution)/shard_map/jit(cholesky)/cholesky | solution.py:28
  173.8 2.3 convolution_subtract_fusion.11
  176.1 11.7 %cholesky.526 = f32[128,128]{1,0:T(8,128)S(1)} custom-call(f32[128,128]{1,0:T(8,128)S(1)} %cholesky.604), custom_call_target="Cholesky" | custom-call | tf_op jit(solution)/shard_map/jit(cholesky)/cholesky | solution.py:28
  189.1 9.8 %custom-call.68 = f32[1,128,128]{1,2,0:T(8,128)S(1)} custom-call(f32[1,128,128]{2,1,0:T(8,128)S(1)} %get-tuple-element.71), custom_call_target="InvertDiagBlocksLowerTriangular" | custom-call | tf_op jit(solution)/shard_map/jit(cholesky)/cholesky | solution.py:28
  199.9 2.1 convolution_subtract_fusion.12
  202.0 11.9 %cholesky.546 = f32[128,128]{1,0:T(8,128)S(1)} custom-call(f32[128,128]{1,0:T(8,128)S(1)} %cholesky.609), custom_call_target="Cholesky" | custom-call | tf_op jit(solution)/shard_map/jit(cholesky)/cholesky | solution.py:28
  215.2 9.8 %custom-call.69 = f32[1,128,128]{1,2,0:T(8,128)S(1)} custom-call(f32[1,128,128]{2,1,0:T(8,128)S(1)} %get-tuple-element.68), custom_call_target="InvertDiagBlocksLowerTriangular" | custom-call | tf_op jit(solution)/shard_map/jit(cholesky)/cholesky | solution.py:28
  227.7 11.7 %cholesky.564 = f32[128,128]{1,0:T(8,128)S(1)} custom-call(f32[128,128]{1,0:T(8,128)S(1)} %convolution_subtract_fusion.13), custom_call_target="Cholesky" | custom-call | tf_op jit(solution)/shard_map/jit(cholesky)/cholesky | solution.py:28
  246.5 6.6 fusion.7
  253.1 23.2 %while.1 = (s32[]{:T(128)}, f32[1024,1024]{1,0:T(8,128)}, s32[8,2]{0,1:T(2,128)S(1)}, f32[8,128,128]{2,1,0:T(8,128)S(1)}, s32[]{:T(128)}) while((s32[]{:T(128)}, f32[1024,1024]{1,0:T(8,128)}, s32[8,2]{0,1:T(2,128)S(1)}, f32[8,128,128]{2,1,0:T(8,128)S(1)}, s32[]{:T(128)}) %tuple.69), condition=%wide.while_cond, body=%wide.while_body.sunk | while | flops 2 | bytes 131189 | solution.py:30
  253.7 2.3 bitcast_dynamic-update-slice_fusion.2
  256.6 2.3 bitcast_dynamic-update-slice_fusion.2
  259.5 2.3 bitcast_dynamic-update-slice_fusion.2
  262.4 2.3 bitcast_dynamic-update-slice_fusion.2
  265.3 2.3 bitcast_dynamic-update-slice_fusion.2
  268.3 2.3 bitcast_dynamic-update-slice_fusion.2
  271.2 2.3 bitcast_dynamic-update-slice_fusion.2
  274.1 2.2 bitcast_dynamic-update-slice_fusion.2
  276.3 79.0 %custom-call.70 = f32[8,128,128]{1,2,0:T(8,128)S(1)} custom-call(f32[8,128,128]{2,1,0:T(8,128)S(1)} %get-tuple-element.16), custom_call_target="InvertDiagBlocksLowerTriangular" | custom-call | tf_op jit(solution)/shard_map/jit(_solve_triangular)/triangular_solve | solution.py:30
  355.3 1.8 constant_dynamic-update-slice_fusion.17
  359.5 2.1 convolution_subtract_fusion.1
  362.3 2.4 convolution_subtract_fusion.6
  365.4 2.8 convolution_subtract_fusion.4
  368.8 3.5 convolution_subtract_fusion.3
  372.9 3.9 convolution_subtract_fusion
  377.4 4.5 convolution_subtract_fusion.2
  382.5 4.0 fusion.75
  389.4 2.0 all_gather.15
  391.4 14.9 %all-gather.5.cloned.1.call-done = f32[1024,1024]{0,1:T(8,128)} async-done(((f32[1024,512]{0,1:T(8,128)}), f32[1024,1024]{0,1:T(8,128)}) %all-gather.5.cloned.1.call-update) | async-done | bytes 4194320 | tf_op jit(solution)/shard_map/all_gather | solution.py:35
  406.3 20.0 %all-gather.7.cloned.1.call-done = f32[1024,1024]{0,1:T(8,128)} async-done(((f32[1024,512]{0,1:T(8,128)}), f32[1024,1024]{0,1:T(8,128)}) %all-gather.7.cloned.1.call-update) | async-done | bytes 4194320 | tf_op jit(solution)/shard_map/all_gather | solution.py:36
  426.2 39.1 %fusion = f32[1056,2112]{1,0:T(8,128)S(1)} fusion(f32[1024,1056]{0,1:T(8,128)} %copy-done.2, f32[1024,64]{0,1:T(8,128)S(1)} %all_gather.15, f32[1024,1024]{0,1:T(8,128)} %all-gather.7.cloned.1.call-done, f32[1024,1024]{0,1:T(8,128)} %all-gather.5.cloned.1.call-done), kind=kOutput, calls=%fused_computation.2 | convolution fusion | flops 27409907712 | bytes 21897216 | tf_op jit(solution)/shard_map/dot_general | solution.py:14
  465.4 3.2 fusion.15
  468.6 2.2 copy-done.1
  470.8 3.7 collective-permute-start.1
  474.5 4.6 collective-permute-start
  480.0 1.8 collective-permute-start.2
  481.8 3.2 dynamic-slice_bitcast_fusion
  485.7 421.3 %psum.7 = f32[32,64]{1,0:T(8,128)S(1)} all-reduce(f32[32,64]{1,0:T(8,128)S(1)} %slice.341), channel_id=1, replica_groups=mesh['tm'=64,'blk'=2] {'tm'}, use_global_device_ids=true, to_apply=%region_16.17 | all-reduce | flops 2048 | bytes 16384 | tf_op jit(solution)/shard_map/psum | solution.py:82
  909.2 5.1 fusion.17
  (89 shorter events, 39.1 us)
Async XLA Ops:
  7.2 1.6 slice-start.2
  7.2 24.1 %all-gather.9.cloned.1.call-start = ((), (), s32[]{:S(2)}) async-start(), calls=%async_computation.3 | async-start | bytes 6291456 | tf_op jit(solution)/shard_map/all_gather | solution.py:27
  16.5 6.6 all-to-all-start
  20.3 385.9 %all-gather.5.cloned.1.call-start = ((), (), s32[]{:S(2)}) async-start(), calls=%async_computation.1 | async-start | bytes 6291456 | tf_op jit(solution)/shard_map/all_gather | solution.py:35
  20.4 6.7 copy-start.3
  41.2 2.0 copy-start
  355.3 7.0 slice-start
  358.9 3.4 slice-start.1
  382.5 4.5 copy-start.2
  387.1 39.2 %all-gather.7.cloned.1.call-start = ((), (), s32[]{:S(2)}) async-start(), calls=%async_computation.2 | async-start | bytes 6291456 | tf_op jit(solution)/shard_map/all_gather | solution.py:36
  465.4 5.4 copy-start.1
  470.8 436.2 %copy-start.4 = (f32[32,64]{1,0:T(8,128)S(1)}, f32[32,64]{1,0:T(8,128)}, u32[]{:S(2)}) copy-start(f32[32,64]{1,0:T(8,128)} %param.7) | copy-start | bytes 24580
  470.8 438.4 %collective-permute-start.1 = (f32[512,1024]{1,0:T(8,128)}, f32[512,1024]{1,0:T(8,128)S(1)}, u32[]{:S(2)}, u32[]{:S(2)}) collective-permute-start(f32[512,1024]{1,0:T(8,128)} %get-tuple-element.30), channel_id=1, source_target_pairs={{0,2},{2,4},{4,6},{6,8},{8,10},{10,12},{12,14},{14,16},{16,18},{18... | collective-permute-start | bytes 6291464 | tf_op jit(solution)/shard_map/ppermute | solution.py:10
  474.5 434.7 %collective-permute-start = (f32[512,1024]{1,0:T(8,128)}, f32[512,1024]{1,0:T(8,128)}, u32[]{:S(2)}, u32[]{:S(2)}) collective-permute-start(f32[512,1024]{1,0:T(8,128)} %get-tuple-element.31), channel_id=1, source_target_pairs={{0,2},{2,4},{4,6},{6,8},{8,10},{10,12},{12,14},{14,16},{16,18},{18... | collective-permute-start | bytes 6291464 | tf_op jit(solution)/shard_map/ppermute | solution.py:10
  480.0 427.6 %collective-permute-start.2 = (f32[32,1024]{1,0:T(8,128)S(1)}, f32[32,1024]{1,0:T(8,128)S(1)}, u32[]{:S(2)}, u32[]{:S(2)}) collective-permute-start(f32[32,1024]{1,0:T(8,128)S(1)} %slice.340), channel_id=1, source_target_pairs={{0,2},{2,4},{4,6},{6,8},{8,10},{10,12},{12,14},{14,16},{16,18},{18... | collective-permute-start | bytes 393224 | tf_op jit(solution)/shard_map/ppermute | solution.py:10
Sparse Core Ops, SparseCore 0:
  10.7 18.7 all-gather.8
  387.2 19.0 all-gather.4
  408.5 17.6 all-gather.6
where the time goes:
time: 927 us; the launch traced here: 922 us
  blocking collectives  423 us (46%)
  other arithmetic  281 us (30%)
  matrix products  89.3 us (10%)
  local copies, waits for them, and re-layouts  56.5 us (6%)
  waiting for transfers between devices  38.4 us (4%)
  between operations  19.6 us (2%)
  starting transfers between devices  14 us (2%)
    psum x1, blocking collectives, local(): corner_out = corner - lax.psum(arrow_arrow, 'tm')  421 us
    another operation x30, other arithmetic, eliminate(): factor = jnp.linalg.cholesky(whole_pivot)  172 us
    another operation x3, other arithmetic, eliminate(): solved = jax.scipy.linalg.solve_triangular(factor, right_hand, lower=True)  85.6 us
    dot_general x1, matrix products, transposed_product(): lax.dot_general(left, right, (((0,), (0,)), ((), ())), precision=lax.Prec...  39.1 us
    another operation x15, matrix products, eliminate(): solved = jax.scipy.linalg.solve_triangular(factor, right_hand, lower=True)  27 us
    another operation x14, matrix products, eliminate(): factor = jnp.linalg.cholesky(whole_pivot)  23.1 us
    another operation x24, local copies, waits for them, and re-layouts  23 us
    all_gather x1, waiting for transfers between devices, eliminate(): lax.all_gather(own_second, 'blk', axis=1, tiled=True)  20 us
  transfers between devices with their start and end apart: 7, of which 3 were waited for; matrix products, arithmetic and copies ran while one was open for 2% of the time, Pallas kernels for 0%

commit v1 on v0

v1 whole, which is shorter than its diff:
```python
import functools

import jax
import jax.numpy as jnp
from jax import lax
from jax.experimental import pallas as pl
from jax.experimental.pallas import tpu as pltpu
from jax.sharding import PartitionSpec as P

MESH = pl.DeviceIdType.MESH
F32 = jnp.float32
BF16 = jnp.bfloat16
NODES = 1024
HALF = 512
FX = 32
BLOCK = 128
STEPS = NODES // BLOCK
ROWS = 2 * HALF + FX
MICRO = 32
LAG = 2


def dot_nt(left, right):
    return lax.dot_general(left, right, (((1,), (1,)), ((), ())), preferred_element_type=F32)


def split(value, parts):
    out = []
    for _ in range(parts):
        piece = value.astype(BF16)
        out.append(piece)
        value = value - piece.astype(F32)
    return out


def left3(value):
    a, b, c = split(value, 3)
    return jnp.concatenate([a, a, b, a, b, c], axis=1)


def right3(value):
    a, b, c = split(value, 3)
    return jnp.concatenate([a, b, a, c, b, a], axis=1)


def left2(value):
    a, b = split(value, 2)
    return jnp.concatenate([a, b, a, b], axis=1)


def right2(value):
    a, b = split(value, 2)
    return jnp.concatenate([a, a, b, b], axis=1)


def factor_inverse(work, done):
    groups = MICRO // 8
    row_id = lax.broadcasted_iota(jnp.int32, (8, 2 * BLOCK), 0)
    twice = lambda value: jnp.concatenate([value, value], axis=1)
    for base in range(0, BLOCK, MICRO):
        rows = [work[base + 8 * g : base + 8 * g + 8, :] for g in range(groups)]
        cols = [
            [jnp.broadcast_to(rows[g][:, base + m : base + m + 1], (8, BLOCK)) for m in range(8 * g + 8)]
            for g in range(groups)
        ]
        final = [jnp.zeros((8, 2 * BLOCK), F32) for _ in range(groups)]
        for j in range(MICRO):
            gj, rj = divmod(j, 8)
            inverse = lax.rsqrt(jnp.broadcast_to(cols[gj][j][rj : rj + 1, :], (8, BLOCK)))
            pivot_row = jnp.broadcast_to(rows[gj][rj : rj + 1, :], (8, 2 * BLOCK)) * twice(inverse)
            final[gj] = jnp.where(row_id == rj, pivot_row, final[gj])
            low = [None] * groups
            for g in range(gj, groups):
                low[g] = cols[g][j] * inverse
                rows[g] = rows[g] - twice(low[g]) * pivot_row
            for m in range(j + 1, MICRO):
                gm, rm = divmod(m, 8)
                factor = jnp.broadcast_to(low[gm][rm : rm + 1, :], (8, BLOCK))
                for g in range(gm, groups):
                    cols[g][m] = cols[g][m] - low[g] * factor
        panel = jnp.concatenate(final, axis=0)
        done[base : base + MICRO, :] = panel
        rest = base + MICRO
        if rest < BLOCK:
            update = lax.dot_general(
                panel[:, :BLOCK],
                panel,
                (((0,), (0,)), ((), ())),
                precision=lax.Precision.HIGHEST,
                preferred_element_type=F32,
            )
            work[rest:, :] = work[rest:, :] - update[rest:, :]


def kernel(
    count,
    diag, coupling, arrow, corner,
    o_pivot, o_left, o_right, o_arrow, o_diag, o_lower, o_upper, o_fixed, o_corner,
    a_mat, r_mat, turn, solved, factor, arrived, sibling, forwarded,
    acc_diag, acc_lower, acc_upper, acc_fixed, acc_corner, fixed_sum,
    cat_left, cat_right, work, done,
    load_sem, out_sem, pair_send, pair_recv,
    next_send, next_recv, sib_send, sib_recv, fwd_send, fwd_recv, sum_send, sum_recv, fin_sem,
):
    p = lax.axis_index("tm")
    c = lax.axis_index("blk")
    other = 1 - c
    nxt = (lax.rem(p + 1, count), c)
    prv = (lax.rem(p + count - 1, count), c)
    sib = (p, other)
    strides = (1, 4, 16)
    spots = [lax.rem(p // s, 4) for s in strides]

    def partner(stage, d):
        spot = spots[stage]
        return (p + (lax.rem(spot + d, 4) - spot) * strides[stage], c)

    own_rows = pl.ds(pl.multiple_of(c * HALF, HALF), HALF)
    other_cols = pl.ds(pl.multiple_of(other * HALF, HALF), HALF)

    barrier = pltpu.get_barrier_semaphore()
    partners = [nxt, prv, sib] + [partner(s, d) for s in range(3) for d in (1, 2, 3)]
    for device in partners:
        pl.semaphore_signal(barrier, inc=1, device_id=device, device_id_type=MESH)

    loads = [
        pltpu.make_async_copy(diag.at[1], a_mat.at[own_rows, :], load_sem.at[0]),
        pltpu.make_async_copy(coupling.at[0, :, own_rows], turn.at[own_rows, :], load_sem.at[1]),
        pltpu.make_async_copy(coupling.at[1], r_mat.at[0:HALF, :], load_sem.at[2]),
        pltpu.make_async_copy(arrow.at[1], r_mat.at[HALF : HALF + FX, :], load_sem.at[3]),
        pltpu.make_async_copy(diag.at[0], acc_diag, load_sem.at[4]),
        pltpu.make_async_copy(arrow.at[0], acc_fixed, load_sem.at[5]),
        pltpu.make_async_copy(corner, fixed_sum, load_sem.at[6]),
    ]
    for copy in loads:
        copy.start()
    pl.semaphore_wait(barrier, len(partners))

    def remote(src, dst, send, recv, device):
        return pltpu.make_async_remote_copy(
            src_ref=src, dst_ref=dst, send_sem=send, recv_sem=recv, device_id=device, device_id_type=MESH
        )

    pairs = [
        remote(diag.at[1], a_mat.at[own_rows, :], pair_send.at[0], pair_recv.at[0], sib),
        remote(coupling.at[0, :, other_cols], turn.at[own_rows, :], pair_send.at[1], pair_recv.at[1], sib),
    ]
    for copy in pairs:
        copy.start()
    r_mat[HALF + FX :, :] = jnp.zeros((HALF, NODES), F32)
    acc_lower[...] = jnp.zeros_like(acc_lower)
    acc_upper[...] = jnp.zeros_like(acc_upper)
    acc_corner[0, spots[0]] = jnp.zeros((FX, 64), F32)
    for copy in loads:
        copy.wait()
    for copy in pairs:
        copy.wait()

    identity = (
        lax.broadcasted_iota(jnp.int32, (BLOCK, BLOCK), 0) == lax.broadcasted_iota(jnp.int32, (BLOCK, BLOCK), 1)
    ).astype(F32)
    open_end = jnp.where(p < count - 1, 1.0, 0.0).astype(F32)

    def to_next(k):
        return remote(solved.at[k], arrived.at[k], next_send.at[k], next_recv.at[k], nxt)

    def to_sibling(k):
        return remote(solved.at[k, HALF:, :], sibling.at[k], sib_send.at[k], sib_recv.at[k], sib)

    def forward(k):
        return remote(arrived.at[k, 0:HALF, :], forwarded.at[k], fwd_send.at[k], fwd_recv.at[k], sib)

    def results(k):
        cols = pl.ds(pl.multiple_of(k * BLOCK, BLOCK), BLOCK)
        return [
            pltpu.make_async_copy(factor.at[k, own_rows, :], o_pivot.at[0, :, cols], out_sem.at[0, k]),
            pltpu.make_async_copy(solved.at[k, HALF + FX :, :], o_left.at[0, :, cols], out_sem.at[1, k]),
            pltpu.make_async_copy(solved.at[k, 0:HALF, :], o_right.at[0, :, cols], out_sem.at[2, k]),
            pltpu.make_async_copy(solved.at[k, HALF : HALF + FX, :], o_arrow.at[0, :, cols], out_sem.at[3, k]),
        ]

    def chain(k):
        cols = pl.ds(pl.multiple_of(k * BLOCK, BLOCK), BLOCK)
        work[:, :BLOCK] = a_mat[cols, cols]
        work[:, BLOCK:] = identity
        factor_inverse(work, done)
        inverse = right3(done[:, BLOCK:])

        def solve_rows(i, carry):
            at = pl.ds(pl.multiple_of(i * 352, 32), 352)
            solved[k, at, :] = dot_nt(left3(r_mat[at, cols]), inverse)
            return carry

        r_mat[0:HALF, cols] = r_mat[0:HALF, cols] * open_end
        r_mat[HALF + FX :, cols] = r_mat[HALF + FX :, cols] + turn[cols, :].T
        lax.fori_loop(0, 3, solve_rows, 0)
        to_next(k).start()
        to_sibling(k).start()

        def factor_rows(i, carry):
            at = pl.ds(pl.multiple_of(i * 256, 256), 256)
            value = dot_nt(left3(a_mat[at, cols]), inverse)
            row = lax.broadcasted_iota(jnp.int32, (256, BLOCK), 0) + i * 256
            col = lax.broadcasted_iota(jnp.int32, (256, BLOCK), 1) + k * BLOCK
            value = jnp.where(row >= col, value, 0.0)
            factor[k, at, :] = value
            a, b, d = split(value, 3)
            cat_left[at, :] = jnp.concatenate([a, a, b, a, b, d], axis=1)
            cat_right[at, :] = jnp.concatenate([a, b, a, d, b, a], axis=1)
            return carry

        lax.fori_loop(0, 4, factor_rows, 0)
        for copy in results(k):
            copy.start()

    def trailing(k):
        def split_rows(i, carry):
            at = pl.ds(pl.multiple_of(i * 352, 32), 352)
            to = pl.ds(pl.multiple_of(i * 352 + NODES, 32), 352)
            cat_left[to, :] = left3(solved[k, at, :])
            return carry

        lax.fori_loop(0, 3, split_rows, 0)

        def columns(j, carry):
            cols = pl.ds(pl.multiple_of(j * 256, 256), 256)
            right = cat_right[cols, :]

            def upper(i, carry):
                at = pl.ds(pl.multiple_of(i * 256, 256), 256)
                a_mat[at, cols] = a_mat[at, cols] - dot_nt(cat_left[at, :], right)
                return carry

            lax.fori_loop(j, 4, upper, 0)

            def lower(i, carry):
                at = pl.ds(pl.multiple_of(i * 352, 32), 352)
                source = pl.ds(pl.multiple_of(i * 352 + NODES, 32), 352)
                r_mat[at, cols] = r_mat[at, cols] - dot_nt(cat_left[source, :], right)
                return carry

            lax.fori_loop(0, 3, lower, 0)
            return carry

        lax.fori_loop((k + 1) // 2, 4, columns, 0)

    def products(held, mine, theirs, first, second):
        top = left2(held[0:HALF, :])
        mid = left2(held[HALF : HALF + FX, :])
        low = left2(held[HALF + FX :, :])
        for right, cols in ((mine, own_rows), (theirs, other_cols)):
            first[:, cols] = first[:, cols] - dot_nt(top, right)
            acc_fixed[:, cols] = acc_fixed[:, cols] - dot_nt(mid, right)
            second[:, cols] = second[:, cols] - dot_nt(low, right)
        return mid

    def stage_copy(stage, d):
        slot = acc_corner.at[stage, spots[stage]]
        return remote(slot, slot, sum_send.at[stage, d - 1], sum_recv.at[stage, d - 1], partner(stage, d))

    def stage_start(stage):
        for d in (1, 2, 3):
            stage_copy(stage, d).start()

    def stage_end(stage):
        for d in (1, 2, 3):
            stage_copy(stage, d).wait()
        return acc_corner[stage, 0] + acc_corner[stage, 1] + acc_corner[stage, 2] + acc_corner[stage, 3]

    def step(k, carry):
        @pl.when(k >= LAG)
        def _():
            back = k - LAG
            to_next(back).wait()
            forward(back).start()

        @pl.when(k < STEPS)
        def _():
            chain(k)

            @pl.when(k < STEPS - 1)
            def _():
                trailing(k)

            to_sibling(k).wait()
            held = solved.at[k]
            near = sibling.at[k]
            mid = products(
                held, right2(held[HALF + FX :, :]), right2(near[FX:, :]), acc_upper, acc_diag
            )
            own = dot_nt(mid, right2(held[HALF : HALF + FX, :]))
            far = dot_nt(mid, right2(near[0:FX, :]))
            both = jnp.where(
                c == 0, jnp.concatenate([own, far], axis=1), jnp.concatenate([far, own], axis=1)
            )
            acc_corner[0, spots[0]] = acc_corner[0, spots[0]] + both

        @pl.when(k == STEPS)
        def _():
            pltpu.make_async_copy(acc_upper, o_upper.at[0], fin_sem.at[0]).start()
            stage_start(0)

        @pl.when(k >= LAG)
        def _():
            back = k - LAG
            forward(back).wait()
            held = arrived.at[back]
            products(held, right2(held[0:HALF, :]), right2(forwarded[back]), acc_diag, acc_lower)

        return carry

    lax.fori_loop(0, STEPS + LAG, step, 0)
    ends = [
        pltpu.make_async_copy(acc_diag, o_diag.at[0], fin_sem.at[1]),
        pltpu.make_async_copy(acc_lower, o_lower.at[0], fin_sem.at[2]),
        pltpu.make_async_copy(acc_fixed, o_fixed.at[0], fin_sem.at[3]),
    ]
    for copy in ends:
        copy.start()
    for stage in (1, 2):
        total = stage_end(stage - 1)
        acc_corner[stage, spots[stage]] = total
        stage_start(stage)
    fixed_sum[...] = fixed_sum[...] - stage_end(2)
    last = pltpu.make_async_copy(fixed_sum, o_corner, fin_sem.at[4])
    last.start()
    ends.append(last)
    ends.append(pltpu.make_async_copy(acc_upper, o_upper.at[0], fin_sem.at[0]))

    def drain(k, carry):
        for copy in results(k):
            copy.wait()
        return carry

    lax.fori_loop(0, STEPS, drain, 0)
    for copy in ends:
        copy.wait()


def local(count, diag_block, coupling, arrow, corner):
    block = jax.ShapeDtypeStruct((1, HALF, NODES), F32)
    strip = jax.ShapeDtypeStruct((1, FX, NODES), F32)
    any_space = pl.BlockSpec(memory_space=pl.ANY)
    dma = pltpu.SemaphoreType.DMA
    return pl.pallas_call(
        functools.partial(kernel, count),
        out_shape=(block, block, block, strip, block, block, block, strip, jax.ShapeDtypeStruct((FX, 64), F32)),
        in_specs=[any_space] * 4,
        out_specs=[any_space] * 9,
        scratch_shapes=[
            pltpu.VMEM((NODES, NODES), F32),
            pltpu.VMEM((ROWS, NODES), F32),
            pltpu.VMEM((NODES, HALF), F32),
            pltpu.VMEM((STEPS, ROWS, BLOCK), F32),
            pltpu.VMEM((STEPS, NODES, BLOCK), F32),
            pltpu.VMEM((STEPS, ROWS, BLOCK), F32),
            pltpu.VMEM((STEPS, HALF + FX, BLOCK), F32),
            pltpu.VMEM((STEPS, HALF, BLOCK), F32),
            pltpu.VMEM((HALF, NODES), F32),
            pltpu.VMEM((HALF, NODES), F32),
            pltpu.VMEM((HALF, NODES), F32),
            pltpu.VMEM((FX, NODES), F32),
            pltpu.VMEM((3, 4, FX, 64), F32),
            pltpu.VMEM((FX, 64), F32),
            pltpu.VMEM((NODES + ROWS, 6 * BLOCK), BF16),
            pltpu.VMEM((NODES, 6 * BLOCK), BF16),
            pltpu.VMEM((BLOCK, 2 * BLOCK), F32),
            pltpu.VMEM((BLOCK, 2 * BLOCK), F32),
            dma((7,)),
            dma((4, STEPS)),
            dma((2,)),
            dma((2,)),
            dma((STEPS,)),
            dma((STEPS,)),
            dma((STEPS,)),
            dma((STEPS,)),
            dma((STEPS,)),
            dma((STEPS,)),
            dma((3, 3)),
            dma((3, 3)),
            dma((5,)),
        ],
        compiler_params=pltpu.CompilerParams(
            collective_id=0, has_side_effects=True, vmem_limit_bytes=58 * 2**20
        ),
        cost_estimate=pl.CostEstimate(flops=30_000_000_000, bytes_accessed=22_000_000, transcendentals=0),
        name="eliminate",
    )(diag_block, coupling, arrow, corner)


def solution(mesh):
    rows = P("tm", "blk", None)
    placed = (rows, rows, rows, P("blk", None))
    return jax.shard_map(
        functools.partial(local, mesh.shape["tm"]),
        mesh=mesh,
        in_specs=placed,
        out_specs=(rows,) * 8 + (P("blk", None),),
        check_vma=False,
    )
```

time: 927 us -> 148 us (0.16)
  blocking collectives: 423 us -> 0 us
  other arithmetic: 281 us -> 0 us
  Pallas kernels: 0 us -> 132 us
  matrix products: 89.3 us -> 0 us
  local copies, waits for them, and re-layouts: 56.5 us -> 15.4 us
  waiting for transfers between devices: 38.4 us -> 0 us
  between operations: 19.6 us -> 0.67 us
  starting transfers between devices: 14 us -> 0 us
    psum x1 -> x0, blocking collectives: 421 us -> none  [local(): corner_out = corner - lax.psum(arrow_arrow, 'tm')]
    another operation x33 -> x0, other arithmetic: 258 us -> none  [the longest x30 172 us: eliminate(): factor = jnp.linalg.cholesky(whole_pivot)]
    pallas_call x0 -> x1, Pallas kernels: none -> 132 us  [local(): pl.pallas_call(functools.partial(kernel, count), out_shape=(block, block,...]
    another operation x29 -> x0, matrix products: 50.2 us -> none  [the longest x15 27 us: eliminate(): solved = jax.scipy.linalg.solve_triangular(factor, right_hand, lower=True)]
    dot_general x1 -> x0, matrix products: 39.1 us -> none  [transposed_product(): lax.dot_general(left, right, (((0,), (0,)), ((), ())), precision=lax.Prec...]
    all_gather x3 -> x0, waiting for transfers between devices: 34.9 us -> none  [the longest x1 20 us: eliminate(): lax.all_gather(own_second, 'blk', axis=1, tiled=True)]
    another operation x33 -> x0, local copies, waits for them, and re-layouts: 25.6 us -> none
    ppermute x3 -> x0, starting transfers between devices: 10.1 us -> none  [shifted(): lax.ppermute(value, axis, [(source, source + steps) for source in range(l...]
  transfers between devices with their start and end apart: 7 -> 0, of which waited for: 3 -> 0; matrix products, arithmetic and copies ran while one was open for 2% -> 0% of each run, Pallas kernels for 0% -> 0%
where the time goes in v1:
time: 148 us
  Pallas kernels  132 us (89%)
  local copies, waits for them, and re-layouts  15.4 us (10%)
    pallas_call x1, Pallas kernels, local(): pl.pallas_call(functools.partial(kernel, count), out_shape=(block, block,...  132 us
    unnamed x25, local copies, waits for them, and re-layouts  15.4 us

profile of v1, /device:TPU:0, one launch (start us, length us, event | category | flops | bytes accessed | tf_op | source)
XLA Modules:
  0.0 147.7 jit_solution(13139980887720518513)
XLA Ops:
  0.6 131.7 %eliminate.1 = (f32[1,512,1024]{2,1,0:T(8,128)}, f32[1,512,1024]{2,1,0:T(8,128)}, f32[1,512,1024]{2,1,0:T(8,128)}, f32[1,32,1024]{2,1,0:T(8,128)}, f32[1,512,102...) custom-call(f32[2,512,1024]{2,1,0:T(8,128)} %diag.1, ...), custom_call_target="tpu_custom_call" | custom-call | flops 30000001024 | bytes 22000000 | tf_op jit(solution)/shard_map/eliminate/pallas_call | solution.py:345
  132.3 0.0 copy-start.4
  132.3 3.3 %copy.22 = f32[1,512,1024]{2,1,0:T(8,128)} copy(f32[1,512,1024]{2,1,0:T(8,128)} %get-tuple-element.18) | data formatting | bytes 4194304
  135.6 0.0 copy-done.4
  135.6 0.0 copy-start.3
  135.6 1.3 copy.23
  136.9 1.0 copy-done.3
  138.0 0.0 copy-start.6
  138.0 0.0 copy-start.2
  138.0 1.3 copy.24
  139.3 0.0 copy-done.6
  139.3 0.7 copy.25
  140.0 0.5 copy-done.2
  140.4 0.0 copy-start.1
  140.4 1.3 copy.26
  141.8 1.0 copy-done.1
  142.8 0.0 copy-start
  142.8 1.3 copy.27
  144.1 1.0 copy-done
  145.1 0.0 copy-start.5
  145.1 0.0 copy-start.7
  145.1 1.3 copy.28
  146.5 0.0 copy-done.5
  146.5 0.7 copy.29
  147.1 0.0 copy-done.7
  147.1 0.6 copy.30
Async XLA Ops:
  132.3 3.3 %copy-start.4 = (f32[1,512,1024]{2,1,0:T(8,128)S(1)}, f32[1,512,1024]{2,1,0:T(8,128)}, u32[]{:S(2)}) copy-start(f32[1,512,1024]{2,1,0:T(8,128)} %get-tuple-element.19) | copy-start | bytes 6291460
  135.6 2.3 %copy-start.3 = (f32[1,512,1024]{2,1,0:T(8,128)S(1)}, f32[1,512,1024]{2,1,0:T(8,128)}, u32[]{:S(2)}) copy-start(f32[1,512,1024]{2,1,0:T(8,128)} %get-tuple-element.20) | copy-start | bytes 6291460
  138.0 1.3 copy-start.6
  138.0 2.5 %copy-start.2 = (f32[1,512,1024]{2,1,0:T(8,128)S(1)}, f32[1,512,1024]{2,1,0:T(8,128)}, u32[]{:S(2)}) copy-start(f32[1,512,1024]{2,1,0:T(8,128)} %get-tuple-element.22) | copy-start | bytes 6291460
  140.4 2.3 %copy-start.1 = (f32[1,512,1024]{2,1,0:T(8,128)S(1)}, f32[1,512,1024]{2,1,0:T(8,128)}, u32[]{:S(2)}) copy-start(f32[1,512,1024]{2,1,0:T(8,128)} %get-tuple-element.23) | copy-start | bytes 6291460
  142.8 2.3 %copy-start = (f32[1,512,1024]{2,1,0:T(8,128)S(1)}, f32[1,512,1024]{2,1,0:T(8,128)}, u32[]{:S(2)}) copy-start(f32[1,512,1024]{2,1,0:T(8,128)} %get-tuple-element.24) | copy-start | bytes 6291460
  145.1 1.3 copy-start.5
  145.1 2.0 %copy-start.7 = (f32[32,64]{1,0:T(8,128)S(1)}, f32[32,64]{1,0:T(8,128)}, u32[]{:S(2)}) copy-start(f32[32,64]{1,0:T(8,128)} %get-tuple-element.26) | copy-start | bytes 24580

commit v2 on v1

v2 whole, which is shorter than its diff:
```python
import functools

import jax
import jax.numpy as jnp
from jax import lax
from jax.experimental import pallas as pl
from jax.experimental.pallas import tpu as pltpu
from jax.sharding import PartitionSpec as P

MESH = pl.DeviceIdType.MESH
F32 = jnp.float32
BF16 = jnp.bfloat16
NODES = 1024
HALF = 512
FX = 32
BLOCK = 128
STEPS = NODES // BLOCK
ROWS = 2 * HALF + FX
MICRO = 32
WIDE = 2 * BLOCK
SUPER = NODES // WIDE
LOW = HALF + FX
CUT = ROWS - 208
RELAY = ROWS - CUT


def dot_nt(left, right):
    return lax.dot_general(left, right, (((1,), (1,)), ((), ())), preferred_element_type=F32)


def split(value, parts):
    out = []
    for _ in range(parts):
        piece = value.astype(BF16)
        out.append(piece)
        value = value - piece.astype(F32)
    return out


def left_terms(value):
    a, b, c = split(value, 3)
    return [a, a, b, a, b, c]


def right_terms(value):
    a, b, c = split(value, 3)
    return [a, b, a, c, b, a]


def joined(terms):
    return jnp.concatenate(terms, axis=1)


def left_pair(first, second):
    a, b = split(jnp.concatenate([first, second], axis=1), 2)
    return joined([a, a, b])


def right_pair(first, second):
    a, b = split(jnp.concatenate([first, second], axis=1), 2)
    return joined([a, b, a])


def factor_inverse(work, done):
    groups = MICRO // 8
    row_id = lax.broadcasted_iota(jnp.int32, (8, 2 * BLOCK), 0)
    twice = lambda value: jnp.concatenate([value, value], axis=1)
    for base in range(0, BLOCK, MICRO):
        rows = [work[base + 8 * g : base + 8 * g + 8, :] for g in range(groups)]
        cols = [
            [jnp.broadcast_to(rows[g][:, base + m : base + m + 1], (8, BLOCK)) for m in range(8 * g + 8)]
            for g in range(groups)
        ]
        final = [jnp.zeros((8, 2 * BLOCK), F32) for _ in range(groups)]
        for j in range(MICRO):
            gj, rj = divmod(j, 8)
            inverse = lax.rsqrt(jnp.broadcast_to(cols[gj][j][rj : rj + 1, :], (8, BLOCK)))
            pivot_row = jnp.broadcast_to(rows[gj][rj : rj + 1, :], (8, 2 * BLOCK)) * twice(inverse)
            final[gj] = jnp.where(row_id == rj, pivot_row, final[gj])
            low = [None] * groups
            for g in range(gj, groups):
                low[g] = cols[g][j] * inverse
                rows[g] = rows[g] - twice(low[g]) * pivot_row
            for m in range(j + 1, MICRO):
                gm, rm = divmod(m, 8)
                factor = jnp.broadcast_to(low[gm][rm : rm + 1, :], (8, BLOCK))
                for g in range(gm, groups):
                    cols[g][m] = cols[g][m] - low[g] * factor
        panel = jnp.concatenate(final, axis=0)
        done[base : base + MICRO, :] = panel
        rest = base + MICRO
        if rest < BLOCK:
            update = lax.dot_general(
                panel[:, :BLOCK],
                panel,
                (((0,), (0,)), ((), ())),
                precision=lax.Precision.HIGHEST,
                preferred_element_type=F32,
            )
            work[rest:, :] = work[rest:, :] - update[rest:, :]


def eliminate(
    count,
    diag, coupling, arrow, corner,
    solved, factor, acc_diag, acc_lower, acc_upper, acc_fixed, fixed_sum,
    a_mat, r_mat, turn, arrived, sibling, forwarded, relay_a, relay_b,
    acc_corner, cat_left, cat_right, work, done,
    a_sem, r_sem, turn_sem, load_sem, a_send, a_recv, turn_send, turn_recv,
    top_send, top_recv, low_send, low_recv, sib_send, sib_recv, fwd_send, fwd_recv,
    hop_send, hop_recv, sum_send, sum_recv,
):
    p = lax.axis_index("tm")
    c = lax.axis_index("blk")
    other = 1 - c
    strides = (1, 4, 16)
    spots = [lax.rem(p // s, 4) for s in strides]
    row_start = p - spots[0]

    def partner(stage, d):
        return (p + (lax.rem(spots[stage] + d, 4) - spots[stage]) * strides[stage], c)

    def in_row(d):
        return row_start + lax.rem(spots[0] + d, 4)

    nxt = (lax.rem(p + 1, count), c)
    prv_tm = lax.rem(p + count - 1, count)
    prv = (prv_tm, c)
    sib = (p, other)
    minus = (in_row(3), c)
    plus = (in_row(1), c)
    hop_to = (jnp.where(spots[0] == 2, lax.rem(row_start + 5, count), minus[0]), c)
    hop_from = (jnp.where(spots[0] == 1, lax.rem(row_start + count - 2, count), plus[0]), c)

    own_rows = pl.ds(pl.multiple_of(c * HALF, HALF), HALF)
    other_cols = pl.ds(pl.multiple_of(other * HALF, HALF), HALF)

    def remote(src, dst, send, recv, device):
        return pltpu.make_async_remote_copy(
            src_ref=src, dst_ref=dst, send_sem=send, recv_sem=recv, device_id=device, device_id_type=MESH
        )

    barrier = pltpu.get_barrier_semaphore()
    senders = [prv, sib, plus, hop_from] + [partner(s, d) for s in range(3) for d in (1, 2, 3)]
    for device in senders:
        pl.semaphore_signal(barrier, inc=1, device_id=device, device_id_type=MESH)

    def wide(s):
        return pl.ds(s * WIDE, WIDE)

    def half_rows(q):
        return pl.ds(pl.multiple_of(c * HALF + q * WIDE, WIDE), WIDE)

    a_loads = [
        pltpu.make_async_copy(diag.at[1, :, wide(s)], a_mat.at[own_rows, wide(s)], a_sem.at[s]) for s in range(SUPER)
    ]
    r_loads = [
        pltpu.make_async_copy(coupling.at[1, :, wide(s)], r_mat.at[0:HALF, wide(s)], r_sem.at[s])
        for s in range(SUPER)
    ]
    turn_loads = [
        pltpu.make_async_copy(coupling.at[0, wide(q), own_rows], turn.at[half_rows(q), :], turn_sem.at[q])
        for q in range(2)
    ]
    loads = [
        pltpu.make_async_copy(arrow.at[1], r_mat.at[HALF:LOW, :], load_sem.at[0]),
        pltpu.make_async_copy(diag.at[0], acc_diag.at[0], load_sem.at[1]),
        pltpu.make_async_copy(arrow.at[0], acc_fixed.at[0], load_sem.at[2]),
        pltpu.make_async_copy(corner, fixed_sum, load_sem.at[3]),
    ]
    a_pairs = [
        remote(diag.at[1, :, wide(s)], a_mat.at[own_rows, wide(s)], a_send.at[s], a_recv.at[s], sib)
        for s in range(SUPER)
    ]
    turn_pairs = [
        remote(coupling.at[0, wide(q), other_cols], turn.at[half_rows(q), :], turn_send.at[q], turn_recv.at[q], sib)
        for q in range(2)
    ]
    early = [a_loads[0], turn_loads[0], r_loads[0], loads[0]]
    late = [a_loads[1], r_loads[1], turn_loads[1], a_loads[2], r_loads[2], a_loads[3], r_loads[3]] + loads[1:]
    early_pairs = [a_pairs[0], turn_pairs[0]]
    late_pairs = [a_pairs[1], turn_pairs[1], a_pairs[2], a_pairs[3]]
    for copy in early:
        copy.start()
    pl.semaphore_wait(barrier, len(senders))
    for copy in early_pairs:
        copy.start()
    for copy in late + late_pairs:
        copy.start()
    r_mat[LOW:, :] = jnp.zeros((HALF, NODES), F32)
    acc_lower[...] = jnp.zeros_like(acc_lower)
    acc_upper[...] = jnp.zeros_like(acc_upper)
    acc_corner[0, spots[0]] = jnp.zeros((FX, 64), F32)
    identity = (
        lax.broadcasted_iota(jnp.int32, (BLOCK, BLOCK), 0) == lax.broadcasted_iota(jnp.int32, (BLOCK, BLOCK), 1)
    ).astype(F32)
    open_end = jnp.where(p < count - 1, 1.0, 0.0).astype(F32)
    for copy in early + early_pairs:
        copy.wait()

    def top_copy(k):
        return remote(solved.at[k, 0:HALF, :], arrived.at[k, 0:HALF, :], top_send.at[k], top_recv.at[k], nxt)

    def low_copy(k):
        return remote(solved.at[k, HALF:CUT, :], arrived.at[k, HALF:CUT, :], low_send.at[k], low_recv.at[k], nxt)

    def hop(stage, k):
        if stage == 0:
            return remote(solved.at[k, CUT:, :], relay_a.at[k], hop_send.at[0, k], hop_recv.at[0, k], minus)
        if stage == 1:
            return remote(relay_a.at[k], relay_b.at[k], hop_send.at[1, k], hop_recv.at[1, k], hop_to)
        return remote(relay_b.at[k], arrived.at[k, CUT:, :], hop_send.at[2, k], hop_recv.at[2, k], minus)

    def to_sibling(k):
        return remote(solved.at[k, HALF:, :], sibling.at[k], sib_send.at[k], sib_recv.at[k], sib)

    def forward(k):
        return remote(arrived.at[k, 0:HALF, :], forwarded.at[k], fwd_send.at[k], fwd_recv.at[k], sib)

    def subtract(target, rows, left, mine, theirs):
        for right, cols in ((mine, own_rows), (theirs, other_cols)):
            target[0, rows, cols] = target[0, rows, cols] - dot_nt(left, right)

    everything = slice(None)

    def local_products(s):
        e, o = 2 * s, 2 * s + 1
        mine = right_pair(solved[e, LOW:, :], solved[o, LOW:, :])
        theirs = right_pair(sibling[e, FX:, :], sibling[o, FX:, :])
        subtract(acc_upper, everything, left_pair(solved[e, 0:HALF, :], solved[o, 0:HALF, :]), mine, theirs)
        subtract(acc_diag, everything, left_pair(solved[e, LOW:, :], solved[o, LOW:, :]), mine, theirs)
        mid = left_pair(solved[e, HALF:LOW, :], solved[o, HALF:LOW, :])
        subtract(acc_fixed, everything, mid, mine, theirs)
        own = dot_nt(mid, right_pair(solved[e, HALF:LOW, :], solved[o, HALF:LOW, :]))
        far = dot_nt(mid, right_pair(sibling[e, 0:FX, :], sibling[o, 0:FX, :]))
        both = jnp.where(c == 0, joined([own, far]), joined([far, own]))
        acc_corner[0, spots[0]] = acc_corner[0, spots[0]] + both

    def arrived_sides(s):
        e, o = 2 * s, 2 * s + 1
        return (
            right_pair(arrived[e, 0:HALF, :], arrived[o, 0:HALF, :]),
            right_pair(forwarded[e], forwarded[o]),
        )

    def arrived_top(s, mine, theirs):
        e, o = 2 * s, 2 * s + 1
        subtract(acc_diag, everything, left_pair(arrived[e, 0:HALF, :], arrived[o, 0:HALF, :]), mine, theirs)

    def arrived_low(s, mine, theirs):
        e, o = 2 * s, 2 * s + 1
        subtract(acc_lower, everything, left_pair(arrived[e, LOW:, :], arrived[o, LOW:, :]), mine, theirs)
        subtract(acc_fixed, everything, left_pair(arrived[e, HALF:LOW, :], arrived[o, HALF:LOW, :]), mine, theirs)

    def half_step(s, h):
        k = 2 * s + h
        cols = pl.ds(pl.multiple_of(k * BLOCK, BLOCK), BLOCK)
        after = pl.ds(pl.multiple_of((2 * s + 1) * BLOCK, BLOCK), BLOCK)
        work[:, :BLOCK] = a_mat[cols, cols]
        work[:, BLOCK:] = identity
        factor_inverse(work, done)
        inverse = joined(right_terms(done[:, BLOCK:]))
        if h == 0:
            beside = joined(right_terms(dot_nt(joined(left_terms(a_mat[after, cols])), inverse)))

        r_mat[0:HALF, cols] = r_mat[0:HALF, cols] * open_end
        r_mat[LOW:, cols] = r_mat[LOW:, cols] + turn[cols, :].T
        value = dot_nt(joined(left_terms(r_mat[:, cols])), inverse)
        solved[k] = value
        top_copy(k).start()
        to_sibling(k).start()

        low_copy(k).start()
        hop(0, k).start()

        terms = left_terms(value)
        for t in range(6):
            cat_left[NODES:, t * WIDE + h * BLOCK : t * WIDE + (h + 1) * BLOCK] = terms[t]
        if h == 0:
            r_mat[:, after] = r_mat[:, after] - dot_nt(joined(terms), beside)

        def factor_rows(i, carry):
            at = pl.ds(pl.multiple_of(i * WIDE, WIDE), WIDE)
            value = dot_nt(joined(left_terms(a_mat[at, cols])), inverse)
            row = lax.broadcasted_iota(jnp.int32, (WIDE, BLOCK), 0) + i * WIDE
            col = lax.broadcasted_iota(jnp.int32, (WIDE, BLOCK), 1) + k * BLOCK
            value = jnp.where(row >= col, value, 0.0)

            @pl.when(i // 2 == c)
            def _():
                factor[k, pl.ds(pl.multiple_of((i - 2 * c) * WIDE, WIDE), WIDE), :] = value

            a, b, d = split(value, 3)
            for t, (x, y) in enumerate(zip([a, a, b, a, b, d], [a, b, a, d, b, a])):
                cat_left[at, t * WIDE + h * BLOCK : t * WIDE + (h + 1) * BLOCK] = x
                cat_right[at, t * WIDE + h * BLOCK : t * WIDE + (h + 1) * BLOCK] = y
            if h == 0:
                a_mat[at, after] = a_mat[at, after] - dot_nt(joined([a, a, b, a, b, d]), beside)
            return carry

        lax.fori_loop(s, SUPER, factor_rows, 0)

        def clear_rows(i, carry):
            @pl.when(i // 2 == c)
            def _():
                factor[k, pl.ds(pl.multiple_of((i - 2 * c) * WIDE, WIDE), WIDE), :] = jnp.zeros((WIDE, BLOCK), F32)

            return carry

        lax.fori_loop(0, s, clear_rows, 0)
        service(k)

    def pass_on(k):
        top_copy(k).wait()
        forward(k).start()

    def second_hop(k):
        hop(0, k).wait()
        hop(1, k).start()

    def third_hop(k):
        hop(1, k).wait()
        hop(2, k).start()

    def service(k):
        @pl.when(k >= 1)
        def _():
            second_hop(k - 1)

        @pl.when(k >= 2)
        def _():
            third_hop(k - 2)
            pass_on(k - 2)

    def trailing(s):
        def columns(j, carry):
            cols = pl.ds(pl.multiple_of(j * WIDE, WIDE), WIDE)
            right = cat_right[cols, :]

            def lower(i, carry):
                at = pl.ds(pl.multiple_of(i * WIDE, WIDE), WIDE)
                a_mat[at, cols] = a_mat[at, cols] - dot_nt(cat_left[at, :], right)
                return carry

            lax.fori_loop(j, SUPER, lower, 0)
            r_mat[:, cols] = r_mat[:, cols] - dot_nt(cat_left[NODES:, :], right)
            return carry

        lax.fori_loop(s + 1, SUPER, columns, 0)

    def super_step(s, carry):
        half_step(s, 0)
        half_step(s, 1)

        @pl.when(s == 0)
        def _():
            for copy in late + late_pairs:
                copy.wait()

        trailing(s)
        return carry

    lax.fori_loop(0, SUPER, super_step, 0)

    def stage_copy(stage, d):
        slot = acc_corner.at[stage, spots[stage]]
        return remote(slot, slot, sum_send.at[stage, d - 1], sum_recv.at[stage, d - 1], partner(stage, d))

    def stage_start(stage):
        for d in (1, 2, 3):
            stage_copy(stage, d).start()

    def stage_end(stage):
        for d in (1, 2, 3):
            stage_copy(stage, d).wait()
        return acc_corner[stage, 0] + acc_corner[stage, 1] + acc_corner[stage, 2] + acc_corner[stage, 3]

    def own(s, carry):
        to_sibling(2 * s).wait()
        to_sibling(2 * s + 1).wait()
        local_products(s)
        return carry

    def received(s, carry):
        for k in (2 * s, 2 * s + 1):
            forward(k).wait()
            low_copy(k).wait()
            hop(2, k).wait()
        mine, theirs = arrived_sides(s)
        arrived_top(s, mine, theirs)
        arrived_low(s, mine, theirs)
        return carry

    def next_stage(stage):
        total = stage_end(stage)
        acc_corner[stage + 1, spots[stage + 1]] = total
        stage_start(stage + 1)

    lax.fori_loop(0, 1, own, 0)
    second_hop(STEPS - 1)
    third_hop(STEPS - 2)
    lax.fori_loop(1, 3, own, 0)
    third_hop(STEPS - 1)
    lax.fori_loop(3, 4, own, 0)
    stage_start(0)
    lax.fori_loop(0, 2, received, 0)
    next_stage(0)
    pass_on(STEPS - 2)
    lax.fori_loop(2, 3, received, 0)
    next_stage(1)
    pass_on(STEPS - 1)
    fixed_sum[...] = fixed_sum[...] - stage_end(2)
    lax.fori_loop(3, 4, received, 0)


def store(
    solved, factor, acc_diag, acc_lower, acc_upper, acc_fixed, fixed_sum,
    o_pivot, o_left, o_right, o_arrow, o_diag, o_lower, o_upper, o_fixed, o_corner, sem,
):
    copies = [
        (acc_diag, o_diag), (acc_lower, o_lower), (acc_upper, o_upper), (acc_fixed, o_fixed), (fixed_sum, o_corner),
    ]
    for k in range(STEPS):
        cols = pl.ds(k * BLOCK, BLOCK)
        copies += [
            (factor.at[k], o_pivot.at[0, :, cols]),
            (solved.at[k, LOW:, :], o_left.at[0, :, cols]),
            (solved.at[k, 0:HALF, :], o_right.at[0, :, cols]),
            (solved.at[k, HALF:LOW, :], o_arrow.at[0, :, cols]),
        ]
    copies = [pltpu.make_async_copy(a, b, sem.at[n]) for n, (a, b) in enumerate(copies)]
    for copy in copies:
        copy.start()
    for copy in copies:
        copy.wait()


def local(count, diag_block, coupling, arrow, corner):
    def shape(*dims):
        return jax.ShapeDtypeStruct(dims, F32)

    block = shape(1, HALF, NODES)
    strip = shape(1, FX, NODES)
    fixed = shape(FX, 64)
    any_space = pl.BlockSpec(memory_space=pl.ANY)
    hbm_space = pl.BlockSpec(memory_space=pltpu.HBM)
    vmem_space = pl.BlockSpec(memory_space=pltpu.VMEM)
    dma = pltpu.SemaphoreType.DMA
    held = pl.pallas_call(
        functools.partial(eliminate, count),
        out_shape=(shape(STEPS, ROWS, BLOCK), shape(STEPS, HALF, BLOCK), block, block, block, strip, fixed),
        in_specs=[hbm_space] * 4,
        out_specs=[vmem_space] * 7,
        scratch_shapes=[
            pltpu.VMEM((NODES, NODES), F32),
            pltpu.VMEM((ROWS, NODES), F32),
            pltpu.VMEM((NODES, HALF), F32),
            pltpu.VMEM((STEPS, ROWS, BLOCK), F32),
            pltpu.VMEM((STEPS, LOW, BLOCK), F32),
            pltpu.VMEM((STEPS, HALF, BLOCK), F32),
            pltpu.VMEM((STEPS, RELAY, BLOCK), F32),
            pltpu.VMEM((STEPS, RELAY, BLOCK), F32),
            pltpu.VMEM((3, 4, FX, 64), F32),
            pltpu.VMEM((NODES + ROWS, 6 * WIDE), BF16),
            pltpu.VMEM((NODES, 6 * WIDE), BF16),
            pltpu.VMEM((BLOCK, 2 * BLOCK), F32),
            pltpu.VMEM((BLOCK, 2 * BLOCK), F32),
            dma((SUPER,)), dma((SUPER,)), dma((2,)), dma((4,)),
            dma((SUPER,)), dma((SUPER,)), dma((2,)), dma((2,)),
            dma((STEPS,)), dma((STEPS,)), dma((STEPS,)), dma((STEPS,)),
            dma((STEPS,)), dma((STEPS,)), dma((STEPS,)), dma((STEPS,)),
            dma((3, STEPS)), dma((3, STEPS)), dma((3, 3)), dma((3, 3)),
        ],
        compiler_params=pltpu.CompilerParams(
            collective_id=0, has_side_effects=True, vmem_limit_bytes=40 * 2**20
        ),
        cost_estimate=pl.CostEstimate(flops=30_000_000_000, bytes_accessed=22_000_000, transcendentals=0),
        name="eliminate",
    )(*[pltpu.with_memory_space_constraint(x, pltpu.HBM) for x in (diag_block, coupling, arrow, corner)])
    return pl.pallas_call(
        store,
        out_shape=(block, block, block, strip, block, block, block, strip, fixed),
        in_specs=[vmem_space] * 7,
        out_specs=[any_space] * 9,
        scratch_shapes=[dma((5 + 4 * STEPS,))],
        compiler_params=pltpu.CompilerParams(vmem_limit_bytes=16 * 2**20),
        name="store",
    )(*held)


def solution(mesh):
    rows = P("tm", "blk", None)
    placed = (rows, rows, rows, P("blk", None))
    return jax.shard_map(
        functools.partial(local, mesh.shape["tm"]),
        mesh=mesh,
        in_specs=placed,
        out_specs=(rows,) * 8 + (P("blk", None),),
        check_vma=False,
    )
```

time: 148 us -> 110 us (0.74)
  Pallas kernels: 132 us -> 109 us
  local copies, waits for them, and re-layouts: 15.4 us -> 0 us
    pallas_call x1 -> x2, Pallas kernels: 132 us -> 109 us  [the longest x1 104 us: local(): pl.pallas_call(functools.partial(eliminate, count), out_shape=(shape(STEP...]
    unnamed x25 -> x0, local copies, waits for them, and re-layouts: 15.4 us -> none
where the time goes in v2:
time: 110 us
  Pallas kernels  109 us (99%)
    pallas_call x1, Pallas kernels, local(): pl.pallas_call(functools.partial(eliminate, count), out_shape=(shape(STEP...  104 us
    pallas_call x1, Pallas kernels, local(): pl.pallas_call(store, out_shape=(block, block, block, strip, block, block...  4.93 us

profile of v2, /device:TPU:0, one launch (start us, length us, event | category | flops | bytes accessed | tf_op | source)
XLA Modules:
  0.0 109.7 jit_solution(2490941295759983276)
XLA Ops:
  0.6 103.9 %eliminate.1 = (f32[8,1056,128]{2,1,0:T(8,128)S(1)}, f32[8,512,128]{2,1,0:T(8,128)S(1)}, f32[1,512,1024]{2,1,0:T(8,128)S(1)}, f32[1,512,1024]{2,1,0:T(8,128)S(1)...) custom-call(f32[2,512,1024]{2,1,0:T(8,128)} %diag.1, f32[2,512,1024]{2,1,0:T(8,128)} %coupling.1, ...), custom_call_target="tpu_custom_call" | custom-call | flops 30000001024 | bytes 22000000 | tf_op jit(solution)/shard_map/eliminate/pallas_call | solution.py:449
  104.6 4.9 %store.1 = (f32[1,512,1024]{2,1,0:T(8,128)}, f32[1,512,1024]{2,1,0:T(8,128)}, f32[1,512,1024]{2,1,0:T(8,128)}, f32[1,32,1024]{2,1,0:T(8,128)}, f32[1,512,1024]{2...) custom-call(f32[8,1056,128]{2,1,0:T(8,128)S(1)} %get-tuple-element.1, ...), custom_call_target="tpu_custom_call" | custom-call | tf_op jit(solution)/shard_map/store/pallas_call | solution.py:480

commit v3 on v2

--- a/solution.py
+++ b/solution.py
@@ -20,7 +20,7 @@
 WIDE = 2 * BLOCK
 SUPER = NODES // WIDE
 LOW = HALF + FX
-CUT = ROWS - 208
+CUT = ROWS - 256
 RELAY = ROWS - CUT
 
 
@@ -37,12 +37,18 @@
     return out
 
 
-def left_terms(value):
+def left_terms(value, parts=3):
+    if parts == 2:
+        a, b = split(value, 2)
+        return [a, a, b]
     a, b, c = split(value, 3)
     return [a, a, b, a, b, c]
 
 
-def right_terms(value):
+def right_terms(value, parts=3):
+    if parts == 2:
+        a, b = split(value, 2)
+        return [a, b, a]
     a, b, c = split(value, 3)
     return [a, b, a, c, b, a]
 
@@ -52,17 +58,16 @@
 
 
 def left_pair(first, second):
-    a, b = split(jnp.concatenate([first, second], axis=1), 2)
-    return joined([a, a, b])
+    return joined(left_terms(joined([first, second]), 2))
 
 
 def right_pair(first, second):
-    a, b = split(jnp.concatenate([first, second], axis=1), 2)
-    return joined([a, b, a])
-
-
-def factor_inverse(work, done):
+    return joined(right_terms(joined([first, second]), 2))
+
+
+def factor_inverse(work, done, tasks=(), every=16):
     groups = MICRO // 8
+    tasks = list(tasks)
     row_id = lax.broadcasted_iota(jnp.int32, (8, 2 * BLOCK), 0)
     twice = lambda value: jnp.concatenate([value, value], axis=1)
     for base in range(0, BLOCK, MICRO):
@@ -73,6 +78,8 @@
         ]
         final = [jnp.zeros((8, 2 * BLOCK), F32) for _ in range(groups)]
         for j in range(MICRO):
+            if tasks and (base + j) % every == every - 1:
+                tasks.pop(0)()
             gj, rj = divmod(j, 8)
             inverse = lax.rsqrt(jnp.broadcast_to(cols[gj][j][rj : rj + 1, :], (8, BLOCK)))
             pivot_row = jnp.broadcast_to(rows[gj][rj : rj + 1, :], (8, 2 * BLOCK)) * twice(inverse)
@@ -98,6 +105,8 @@
                 preferred_element_type=F32,
             )
             work[rest:, :] = work[rest:, :] - update[rest:, :]
+    for task in tasks:
+        task()
 
 
 def eliminate(
@@ -105,7 +114,7 @@
     diag, coupling, arrow, corner,
     solved, factor, acc_diag, acc_lower, acc_upper, acc_fixed, fixed_sum,
     a_mat, r_mat, turn, arrived, sibling, forwarded, relay_a, relay_b,
-    acc_corner, cat_left, cat_right, work, done,
+    acc_corner, cat_left, cat_right, cat_rows, work, done,
     a_sem, r_sem, turn_sem, load_sem, a_send, a_recv, turn_send, turn_recv,
     top_send, top_recv, low_send, low_recv, sib_send, sib_recv, fwd_send, fwd_recv,
     hop_send, hop_recv, sum_send, sum_recv,
@@ -217,40 +226,66 @@
     def forward(k):
         return remote(arrived.at[k, 0:HALF, :], forwarded.at[k], fwd_send.at[k], fwd_recv.at[k], sib)
 
-    def subtract(target, rows, left, mine, theirs):
-        for right, cols in ((mine, own_rows), (theirs, other_cols)):
-            target[0, rows, cols] = target[0, rows, cols] - dot_nt(left, right)
-
-    everything = slice(None)
-
-    def local_products(s):
+    def tile(base, q):
+        return pl.ds(pl.multiple_of(base * HALF + q * WIDE, WIDE), WIDE)
+
+    def product_tasks(top, low, mine, theirs, first, second):
+        tasks = []
+        for right, base in ((mine, c), (theirs, other)):
+            for q in range(2):
+                piece = right[q * WIDE : (q + 1) * WIDE, :]
+                cols = tile(base, q)
+
+                def upper(piece=piece, cols=cols):
+                    first[0, :, cols] = first[0, :, cols] - dot_nt(top, piece)
+
+                def lower(piece=piece, cols=cols):
+                    value = dot_nt(low, piece)
+                    acc_fixed[0, :, cols] = acc_fixed[0, :, cols] - value[0:FX, :]
+                    second[0, :, cols] = second[0, :, cols] - value[FX:, :]
+
+                tasks += [upper, lower]
+        return tasks
+
+    def local_tasks(s):
         e, o = 2 * s, 2 * s + 1
-        mine = right_pair(solved[e, LOW:, :], solved[o, LOW:, :])
-        theirs = right_pair(sibling[e, FX:, :], sibling[o, FX:, :])
-        subtract(acc_upper, everything, left_pair(solved[e, 0:HALF, :], solved[o, 0:HALF, :]), mine, theirs)
-        subtract(acc_diag, everything, left_pair(solved[e, LOW:, :], solved[o, LOW:, :]), mine, theirs)
-        mid = left_pair(solved[e, HALF:LOW, :], solved[o, HALF:LOW, :])
-        subtract(acc_fixed, everything, mid, mine, theirs)
-        own = dot_nt(mid, right_pair(solved[e, HALF:LOW, :], solved[o, HALF:LOW, :]))
-        far = dot_nt(mid, right_pair(sibling[e, 0:FX, :], sibling[o, 0:FX, :]))
-        both = jnp.where(c == 0, joined([own, far]), joined([far, own]))
-        acc_corner[0, spots[0]] = acc_corner[0, spots[0]] + both
-
-    def arrived_sides(s):
+        low = cat_rows[HALF:, :]
+        far = right_pair(sibling[e], sibling[o])
+        near = joined([low[:, 0:WIDE], low[:, 2 * WIDE :], low[:, 0:WIDE]])
+
+        def fixed():
+            mid = low[0:FX, :]
+            own, their = dot_nt(mid, near[0:FX, :]), dot_nt(mid, far[0:FX, :])
+            both = jnp.where(c == 0, joined([own, their]), joined([their, own]))
+            acc_corner[0, spots[0]] = acc_corner[0, spots[0]] + both
+
+        return product_tasks(cat_rows[0:HALF, :], low, near[FX:, :], far[FX:, :], acc_upper, acc_diag) + [fixed]
+
+    def received_tasks(s):
         e, o = 2 * s, 2 * s + 1
-        return (
+        return product_tasks(
+            left_pair(arrived[e, 0:HALF, :], arrived[o, 0:HALF, :]),
+            left_pair(arrived[e, HALF:, :], arrived[o, HALF:, :]),
             right_pair(arrived[e, 0:HALF, :], arrived[o, 0:HALF, :]),
             right_pair(forwarded[e], forwarded[o]),
+            acc_diag,
+            acc_lower,
         )
 
-    def arrived_top(s, mine, theirs):
-        e, o = 2 * s, 2 * s + 1
-        subtract(acc_diag, everything, left_pair(arrived[e, 0:HALF, :], arrived[o, 0:HALF, :]), mine, theirs)
-
-    def arrived_low(s, mine, theirs):
-        e, o = 2 * s, 2 * s + 1
-        subtract(acc_lower, everything, left_pair(arrived[e, LOW:, :], arrived[o, LOW:, :]), mine, theirs)
-        subtract(acc_fixed, everything, left_pair(arrived[e, HALF:LOW, :], arrived[o, HALF:LOW, :]), mine, theirs)
+    def received_block_tasks(k):
+        return product_tasks(
+            joined(left_terms(arrived[k, 0:HALF, :], 2)),
+            joined(left_terms(arrived[k, HALF:, :], 2)),
+            joined(right_terms(arrived[k, 0:HALF, :], 2)),
+            joined(right_terms(forwarded[k], 2)),
+            acc_diag,
+            acc_lower,
+        )
+
+    def await_received(k):
+        forward(k).wait()
+        low_copy(k).wait()
+        hop(2, k).wait()
 
     def half_step(s, h):
         k = 2 * s + h
@@ -258,14 +293,36 @@
         after = pl.ds(pl.multiple_of((2 * s + 1) * BLOCK, BLOCK), BLOCK)
         work[:, :BLOCK] = a_mat[cols, cols]
         work[:, BLOCK:] = identity
-        factor_inverse(work, done)
+        if h == 0:
+
+            @pl.when(s == 0)
+            def _():
+                factor_inverse(work, done)
+
+            @pl.when(s >= 1)
+            def _():
+                to_sibling(2 * s - 2).wait()
+                to_sibling(2 * s - 1).wait()
+                factor_inverse(work, done, local_tasks(s - 1))
+        else:
+
+            @pl.when(s < 2)
+            def _():
+                factor_inverse(work, done)
+
+            @pl.when(s >= 2)
+            def _():
+                await_received(2 * s - 4)
+                await_received(2 * s - 3)
+                factor_inverse(work, done, received_tasks(s - 2))
+
         inverse = joined(right_terms(done[:, BLOCK:]))
         if h == 0:
             beside = joined(right_terms(dot_nt(joined(left_terms(a_mat[after, cols])), inverse)))
 
         r_mat[0:HALF, cols] = r_mat[0:HALF, cols] * open_end
         r_mat[LOW:, cols] = r_mat[LOW:, cols] + turn[cols, :].T
-        value = dot_nt(joined(left_terms(r_mat[:, cols])), inverse)
+        value = dot_nt(joined(left_terms(r_mat[:, cols], 2)), inverse[:, : 3 * BLOCK])
         solved[k] = value
         top_copy(k).start()
         to_sibling(k).start()
@@ -273,11 +330,11 @@
         low_copy(k).start()
         hop(0, k).start()
 
-        terms = left_terms(value)
-        for t in range(6):
-            cat_left[NODES:, t * WIDE + h * BLOCK : t * WIDE + (h + 1) * BLOCK] = terms[t]
+        terms = left_terms(value, 2)
+        for t in range(3):
+            cat_rows[:, t * WIDE + h * BLOCK : t * WIDE + (h + 1) * BLOCK] = terms[t]
         if h == 0:
-            r_mat[:, after] = r_mat[:, after] - dot_nt(joined(terms), beside)
+            r_mat[:, after] = r_mat[:, after] - dot_nt(joined(terms), beside[:, : 3 * BLOCK])
 
         def factor_rows(i, carry):
             at = pl.ds(pl.multiple_of(i * WIDE, WIDE), WIDE)
@@ -343,7 +400,7 @@
                 return carry
 
             lax.fori_loop(j, SUPER, lower, 0)
-            r_mat[:, cols] = r_mat[:, cols] - dot_nt(cat_left[NODES:, :], right)
+            r_mat[:, cols] = r_mat[:, cols] - dot_nt(cat_rows[...], right[:, : 3 * WIDE])
             return carry
 
         lax.fori_loop(s + 1, SUPER, columns, 0)
@@ -375,42 +432,34 @@
             stage_copy(stage, d).wait()
         return acc_corner[stage, 0] + acc_corner[stage, 1] + acc_corner[stage, 2] + acc_corner[stage, 3]
 
-    def own(s, carry):
-        to_sibling(2 * s).wait()
-        to_sibling(2 * s + 1).wait()
-        local_products(s)
-        return carry
-
-    def received(s, carry):
-        for k in (2 * s, 2 * s + 1):
-            forward(k).wait()
-            low_copy(k).wait()
-            hop(2, k).wait()
-        mine, theirs = arrived_sides(s)
-        arrived_top(s, mine, theirs)
-        arrived_low(s, mine, theirs)
-        return carry
-
     def next_stage(stage):
         total = stage_end(stage)
         acc_corner[stage + 1, spots[stage + 1]] = total
         stage_start(stage + 1)
 
-    lax.fori_loop(0, 1, own, 0)
     second_hop(STEPS - 1)
     third_hop(STEPS - 2)
-    lax.fori_loop(1, 3, own, 0)
+    to_sibling(STEPS - 2).wait()
+    to_sibling(STEPS - 1).wait()
+    for task in local_tasks(SUPER - 1):
+        task()
+    stage_start(0)
     third_hop(STEPS - 1)
-    lax.fori_loop(3, 4, own, 0)
-    stage_start(0)
-    lax.fori_loop(0, 2, received, 0)
+    await_received(STEPS - 4)
+    await_received(STEPS - 3)
+    for task in received_tasks(SUPER - 2):
+        task()
     next_stage(0)
     pass_on(STEPS - 2)
-    lax.fori_loop(2, 3, received, 0)
+    await_received(STEPS - 2)
+    for task in received_block_tasks(STEPS - 2):
+        task()
     next_stage(1)
     pass_on(STEPS - 1)
     fixed_sum[...] = fixed_sum[...] - stage_end(2)
-    lax.fori_loop(3, 4, received, 0)
+    await_received(STEPS - 1)
+    for task in received_block_tasks(STEPS - 1):
+        task()
 
 
 def store(
@@ -461,8 +510,9 @@
             pltpu.VMEM((STEPS, RELAY, BLOCK), F32),
             pltpu.VMEM((STEPS, RELAY, BLOCK), F32),
             pltpu.VMEM((3, 4, FX, 64), F32),
-            pltpu.VMEM((NODES + ROWS, 6 * WIDE), BF16),
             pltpu.VMEM((NODES, 6 * WIDE), BF16),
+            pltpu.VMEM((NODES, 6 * WIDE), BF16),
+            pltpu.VMEM((ROWS, 3 * WIDE), BF16),
             pltpu.VMEM((BLOCK, 2 * BLOCK), F32),
             pltpu.VMEM((BLOCK, 2 * BLOCK), F32),
             dma((SUPER,)), dma((SUPER,)), dma((2,)), dma((4,)),

time: 110 us -> 105 us (0.955)
  Pallas kernels: 109 us -> 104 us
    pallas_call x1, Pallas kernels: 104 us -> 99.5 us  [local(): pl.pallas_call(functools.partial(eliminate, count), out_shape=(shape(STEP...]
where the time goes in v3:
time: 105 us
  Pallas kernels  104 us (99%)
    pallas_call x1, Pallas kernels, local(): pl.pallas_call(functools.partial(eliminate, count), out_shape=(shape(STEP...  99.5 us
    pallas_call x1, Pallas kernels, local(): pl.pallas_call(store, out_shape=(block, block, block, strip, block, block...  4.93 us

profile of v3, /device:TPU:0, one launch (start us, length us, event | category | flops | bytes accessed | tf_op | source)
XLA Modules:
  0.0 105.2 jit_solution(18091707090276223211)
XLA Ops:
  0.6 99.5 %eliminate.1 = (f32[8,1056,128]{2,1,0:T(8,128)S(1)}, f32[8,512,128]{2,1,0:T(8,128)S(1)}, f32[1,512,1024]{2,1,0:T(8,128)S(1)}, f32[1,512,1024]{2,1,0:T(8,128)S(1)...) custom-call(f32[2,512,1024]{2,1,0:T(8,128)} %diag.1, f32[2,512,1024]{2,1,0:T(8,128)} %coupling.1, ...), custom_call_target="tpu_custom_call" | custom-call | flops 30000001024 | bytes 22000000 | tf_op jit(solution)/shard_map/eliminate/pallas_call | solution.py:498
  100.1 4.9 %store.1 = (f32[1,512,1024]{2,1,0:T(8,128)}, f32[1,512,1024]{2,1,0:T(8,128)}, f32[1,512,1024]{2,1,0:T(8,128)}, f32[1,32,1024]{2,1,0:T(8,128)}, f32[1,512,1024]{2...) custom-call(f32[8,1056,128]{2,1,0:T(8,128)S(1)} %get-tuple-element.1, ...), custom_call_target="tpu_custom_call" | custom-call | tf_op jit(solution)/shard_map/store/pallas_call | solution.py:530

commit v4 on v3

--- a/solution.py
+++ b/solution.py
@@ -17,10 +17,11 @@
 STEPS = NODES // BLOCK
 ROWS = 2 * HALF + FX
 MICRO = 32
+IN_FLIGHT = 2
 WIDE = 2 * BLOCK
 SUPER = NODES // WIDE
 LOW = HALF + FX
-CUT = ROWS - 256
+CUT = ROWS - 240
 RELAY = ROWS - CUT
 
 
@@ -114,23 +115,24 @@
     diag, coupling, arrow, corner,
     solved, factor, acc_diag, acc_lower, acc_upper, acc_fixed, fixed_sum,
     a_mat, r_mat, turn, arrived, sibling, forwarded, relay_a, relay_b,
-    acc_corner, cat_left, cat_right, cat_rows, work, done,
+    acc_corner, cat_left, cat_right, cat_rows, work, done, lead, lead_in,
     a_sem, r_sem, turn_sem, load_sem, a_send, a_recv, turn_send, turn_recv,
     top_send, top_recv, low_send, low_recv, sib_send, sib_recv, fwd_send, fwd_recv,
-    hop_send, hop_recv, sum_send, sum_recv,
+    hop_send, hop_recv, sum_send, sum_recv, lead_send, lead_recv,
 ):
     p = lax.axis_index("tm")
     c = lax.axis_index("blk")
     other = 1 - c
-    strides = (1, 4, 16)
+    strides = (16, 4, 1)
     spots = [lax.rem(p // s, 4) for s in strides]
-    row_start = p - spots[0]
+    spot = spots[2]
+    row_start = p - spot
 
     def partner(stage, d):
         return (p + (lax.rem(spots[stage] + d, 4) - spots[stage]) * strides[stage], c)
 
     def in_row(d):
-        return row_start + lax.rem(spots[0] + d, 4)
+        return row_start + lax.rem(spot + d, 4)
 
     nxt = (lax.rem(p + 1, count), c)
     prv_tm = lax.rem(p + count - 1, count)
@@ -138,8 +140,8 @@
     sib = (p, other)
     minus = (in_row(3), c)
     plus = (in_row(1), c)
-    hop_to = (jnp.where(spots[0] == 2, lax.rem(row_start + 5, count), minus[0]), c)
-    hop_from = (jnp.where(spots[0] == 1, lax.rem(row_start + count - 2, count), plus[0]), c)
+    hop_to = (jnp.where(spot == 2, lax.rem(row_start + 5, count), minus[0]), c)
+    hop_from = (jnp.where(spot == 1, lax.rem(row_start + count - 2, count), plus[0]), c)
 
     own_rows = pl.ds(pl.multiple_of(c * HALF, HALF), HALF)
     other_cols = pl.ds(pl.multiple_of(other * HALF, HALF), HALF)
@@ -194,6 +196,11 @@
     pl.semaphore_wait(barrier, len(senders))
     for copy in early_pairs:
         copy.start()
+    raw_top = remote(
+        coupling.at[1, :, pl.ds(0, BLOCK)], arrived.at[0, 0:HALF, :], top_send.at[0], top_recv.at[0], nxt
+    )
+    raw_top.start()
+    lead_copy = remote(lead, lead_in, lead_send, lead_recv, nxt)
     for copy in late + late_pairs:
         copy.start()
     r_mat[LOW:, :] = jnp.zeros((HALF, NODES), F32)
@@ -204,6 +211,7 @@
         lax.broadcasted_iota(jnp.int32, (BLOCK, BLOCK), 0) == lax.broadcasted_iota(jnp.int32, (BLOCK, BLOCK), 1)
     ).astype(F32)
     open_end = jnp.where(p < count - 1, 1.0, 0.0).astype(F32)
+    open_start = jnp.where(p > 0, 1.0, 0.0).astype(F32)
     for copy in early + early_pairs:
         copy.wait()
 
@@ -284,7 +292,7 @@
 
     def await_received(k):
         forward(k).wait()
-        low_copy(k).wait()
+        low_copy(k).wait_recv()
         hop(2, k).wait()
 
     def half_step(s, h):
@@ -324,7 +332,22 @@
         r_mat[LOW:, cols] = r_mat[LOW:, cols] + turn[cols, :].T
         value = dot_nt(joined(left_terms(r_mat[:, cols], 2)), inverse[:, : 3 * BLOCK])
         solved[k] = value
-        top_copy(k).start()
+        @pl.when(k >= IN_FLIGHT)
+        def _():
+            sent(k - IN_FLIGHT)
+
+        if h == 0:
+
+            @pl.when(s == 0)
+            def _():
+                lead[...] = done[:, BLOCK:]
+                lead_copy.start()
+
+            @pl.when(s > 0)
+            def _():
+                top_copy(k).start()
+        else:
+            top_copy(k).start()
         to_sibling(k).start()
 
         low_copy(k).start()
@@ -365,10 +388,21 @@
             return carry
 
         lax.fori_loop(0, s, clear_rows, 0)
-        service(k)
+        if h == 0:
+            service(k)
+        else:
+
+            @pl.when(s < SUPER - 1)
+            def _():
+                service(k)
+
+
+    def sent(k):
+        top_copy(k).wait_send()
+        low_copy(k).wait_send()
 
     def pass_on(k):
-        top_copy(k).wait()
+        top_copy(k).wait_recv()
         forward(k).start()
 
     def second_hop(k):
@@ -387,6 +421,19 @@
         @pl.when(k >= 2)
         def _():
             third_hop(k - 2)
+
+        @pl.when(k == 2)
+        def _():
+            raw_top.wait_recv()
+            lead_copy.wait()
+            raw = arrived[0, 0:HALF, :] * open_start
+            arrived[0, 0:HALF, :] = dot_nt(
+                joined(left_terms(raw, 2)), joined(right_terms(lead_in[...], 2))
+            )
+            forward(0).start()
+
+        @pl.when(k >= 3)
+        def _():
             pass_on(k - 2)
 
     def trailing(s):
@@ -437,29 +484,34 @@
         acc_corner[stage + 1, spots[stage + 1]] = total
         stage_start(stage + 1)
 
-    second_hop(STEPS - 1)
-    third_hop(STEPS - 2)
     to_sibling(STEPS - 2).wait()
     to_sibling(STEPS - 1).wait()
     for task in local_tasks(SUPER - 1):
         task()
     stage_start(0)
-    third_hop(STEPS - 1)
+    second_hop(STEPS - 2)
+    third_hop(STEPS - 3)
+    pass_on(STEPS - 3)
+    second_hop(STEPS - 1)
+    third_hop(STEPS - 2)
     await_received(STEPS - 4)
     await_received(STEPS - 3)
     for task in received_tasks(SUPER - 2):
         task()
-    next_stage(0)
+    third_hop(STEPS - 1)
     pass_on(STEPS - 2)
     await_received(STEPS - 2)
     for task in received_block_tasks(STEPS - 2):
         task()
+    next_stage(0)
+    pass_on(STEPS - 1)
     next_stage(1)
-    pass_on(STEPS - 1)
-    fixed_sum[...] = fixed_sum[...] - stage_end(2)
     await_received(STEPS - 1)
     for task in received_block_tasks(STEPS - 1):
         task()
+    fixed_sum[...] = fixed_sum[...] - stage_end(2)
+    for k in range(STEPS - IN_FLIGHT, STEPS):
+        sent(k)
 
 
 def store(
@@ -515,11 +567,13 @@
             pltpu.VMEM((ROWS, 3 * WIDE), BF16),
             pltpu.VMEM((BLOCK, 2 * BLOCK), F32),
             pltpu.VMEM((BLOCK, 2 * BLOCK), F32),
+            pltpu.VMEM((BLOCK, BLOCK), F32),
+            pltpu.VMEM((BLOCK, BLOCK), F32),
             dma((SUPER,)), dma((SUPER,)), dma((2,)), dma((4,)),
             dma((SUPER,)), dma((SUPER,)), dma((2,)), dma((2,)),
             dma((STEPS,)), dma((STEPS,)), dma((STEPS,)), dma((STEPS,)),
             dma((STEPS,)), dma((STEPS,)), dma((STEPS,)), dma((STEPS,)),
-            dma((3, STEPS)), dma((3, STEPS)), dma((3, 3)), dma((3, 3)),
+            dma((3, STEPS)), dma((3, STEPS)), dma((3, 3)), dma((3, 3)), dma, dma,
         ],
         compiler_params=pltpu.CompilerParams(
             collective_id=0, has_side_effects=True, vmem_limit_bytes=40 * 2**20

time: 105 us -> 102 us (0.971)
  Pallas kernels: 104 us -> 101 us
    pallas_call x1, Pallas kernels: 99.5 us -> 96.2 us  [local(): pl.pallas_call(functools.partial(eliminate, count), out_shape=(shape(STEP...]
where the time goes in v4:
time: 102 us
  Pallas kernels  101 us (99%)
    pallas_call x1, Pallas kernels, local(): pl.pallas_call(functools.partial(eliminate, count), out_shape=(shape(STEP...  96.2 us
    pallas_call x1, Pallas kernels, local(): pl.pallas_call(store, out_shape=(block, block, block, strip, block, block...  4.93 us

profile of v4, /device:TPU:0, one launch (start us, length us, event | category | flops | bytes accessed | tf_op | source)
XLA Modules:
  0.0 102.0 jit_solution(6676063370487927713)
XLA Ops:
  0.6 96.2 %eliminate.1 = (f32[8,1056,128]{2,1,0:T(8,128)S(1)}, f32[8,512,128]{2,1,0:T(8,128)S(1)}, f32[1,512,1024]{2,1,0:T(8,128)S(1)}, f32[1,512,1024]{2,1,0:T(8,128)S(1)...) custom-call(f32[2,512,1024]{2,1,0:T(8,128)} %diag.1, f32[2,512,1024]{2,1,0:T(8,128)} %coupling.1, ...), custom_call_target="tpu_custom_call" | custom-call | flops 30000001024 | bytes 22000000 | tf_op jit(solution)/shard_map/eliminate/pallas_call | solution.py:550
  96.9 4.9 %store.1 = (f32[1,512,1024]{2,1,0:T(8,128)}, f32[1,512,1024]{2,1,0:T(8,128)}, f32[1,512,1024]{2,1,0:T(8,128)}, f32[1,32,1024]{2,1,0:T(8,128)}, f32[1,512,1024]{2...) custom-call(f32[8,1056,128]{2,1,0:T(8,128)S(1)} %get-tuple-element.1, ...), custom_call_target="tpu_custom_call" | custom-call | tf_op jit(solution)/shard_map/store/pallas_call | solution.py:584

commit v5 on v4

--- a/solution.py
+++ b/solution.py
@@ -290,6 +290,27 @@
             acc_lower,
         )
 
+    def last_block(k):
+        sides = (
+            (joined(right_terms(arrived[k, 0:HALF, :], 2)), c),
+            (joined(right_terms(forwarded[k], 2)), other),
+        )
+        top = joined(left_terms(arrived[k, 0:HALF, :], 2))
+        for right, base in sides:
+            for q in range(2):
+                cols = tile(base, q)
+                piece = right[q * WIDE : (q + 1) * WIDE, :]
+                acc_diag[0, :, cols] = acc_diag[0, :, cols] - dot_nt(top, piece)
+        low_copy(k).wait_recv()
+        hop(2, k).wait()
+        low = joined(left_terms(arrived[k, HALF:, :], 2))
+        for right, base in sides:
+            for q in range(2):
+                cols = tile(base, q)
+                value = dot_nt(low, right[q * WIDE : (q + 1) * WIDE, :])
+                acc_fixed[0, :, cols] = acc_fixed[0, :, cols] - value[0:FX, :]
+                acc_lower[0, :, cols] = acc_lower[0, :, cols] - value[FX:, :]
+
     def await_received(k):
         forward(k).wait()
         low_copy(k).wait_recv()
@@ -506,9 +527,8 @@
     next_stage(0)
     pass_on(STEPS - 1)
     next_stage(1)
-    await_received(STEPS - 1)
-    for task in received_block_tasks(STEPS - 1):
-        task()
+    forward(STEPS - 1).wait()
+    last_block(STEPS - 1)
     fixed_sum[...] = fixed_sum[...] - stage_end(2)
     for k in range(STEPS - IN_FLIGHT, STEPS):
         sent(k)

time: 102 us -> 102 us (level)
  no operation moved by 1% of the time
where the time goes in v5:
time: 102 us
  Pallas kernels  101 us (99%)
    pallas_call x1, Pallas kernels, local(): pl.pallas_call(functools.partial(eliminate, count), out_shape=(shape(STEP...  96.2 us
    pallas_call x1, Pallas kernels, local(): pl.pallas_call(store, out_shape=(block, block, block, strip, block, block...  4.93 us

profile of v5, /device:TPU:0, one launch (start us, length us, event | category | flops | bytes accessed | tf_op | source)
XLA Modules:
  0.0 102.0 jit_solution(17187317576506484050)
XLA Ops:
  0.6 96.2 %eliminate.1 = (f32[8,1056,128]{2,1,0:T(8,128)S(1)}, f32[8,512,128]{2,1,0:T(8,128)S(1)}, f32[1,512,1024]{2,1,0:T(8,128)S(1)}, f32[1,512,1024]{2,1,0:T(8,128)S(1)...) custom-call(f32[2,512,1024]{2,1,0:T(8,128)} %diag.1, f32[2,512,1024]{2,1,0:T(8,128)} %coupling.1, ...), custom_call_target="tpu_custom_call" | custom-call | flops 30000001024 | bytes 22000000 | tf_op jit(solution)/shard_map/eliminate/pallas_call | solution.py:570
  96.9 4.9 %store.1 = (f32[1,512,1024]{2,1,0:T(8,128)}, f32[1,512,1024]{2,1,0:T(8,128)}, f32[1,512,1024]{2,1,0:T(8,128)}, f32[1,32,1024]{2,1,0:T(8,128)}, f32[1,512,1024]{2...) custom-call(f32[8,1056,128]{2,1,0:T(8,128)S(1)} %get-tuple-element.1, ...), custom_call_target="tpu_custom_call" | custom-call | tf_op jit(solution)/shard_map/store/pallas_call | solution.py:604
